TPU v7x, 256 devices: a whole 4x4x8 slice. The times are simulated.
256 devices in a mesh: src: 2 (over core), rows: 128 (over z, y, x).
Axes of the slice: x: 4, y: 4, z: 8, core: 2. Of those that a mesh axis runs over, the one named last changes fastest.
Arguments:
- slip_units: int32 [512, 2000], P(None, 'src'), may hold values from 0 to 15
- slip_scales: float32 [512, 16], P(None, 'src'), may hold values from 0.02 to 0.2
- green: bfloat16 [2000, 491520], P('src', 'rows'), may hold values from -0.08944272 to 0.08944272
- coast_gauges: int32 [16384, 8], replicated, may hold values from 0 to 2047
- coast_amps: float32 [16384, 8], replicated, may hold values from 0.05 to 0.3
- coast_counts: int32 [16384], replicated, may hold values from 1 to 8
Outputs:
- onshore: float32 [512, 16384], P('src', 'rows')
Inputs may be any that keep to these rules, and one draw needn't show every extreme that they name: coast_gauges names gauges.
All inputs are finite; a program needn't handle non-finite values.
Results may differ from a plain program's by a relative error of at most 0.0039.
Values may be sent and summed in bfloat16 or wider, within the bound.
A program may use at most 64 MiB of HBM per device.

v0:
```python
import jax
import jax.numpy as jnp
from jax import lax
from jax.sharding import PartitionSpec as P

NT = 240
UBLK = 125


def body(slip_units, slip_scales, green, coast_gauges, coast_amps, coast_counts):
    scenarios = slip_units.shape[0]
    sources_here = slip_units.shape[1]
    block_count = slip_scales.shape[1]
    slip_weights = (
        (
            slip_units.astype(jnp.float32).reshape(scenarios, block_count, UBLK)
            * slip_scales[:, :, None]
        )
        .reshape(scenarios, sources_here)
        .astype(jnp.bfloat16)
    )
    columns = green.shape[1]
    gauge_count = columns // NT
    groups = lax.axis_size("src")
    portion = scenarios // groups
    waveforms = lax.psum_scatter(
        jnp.dot(slip_weights, green, preferred_element_type=jnp.float32).astype(jnp.bfloat16),
        "src",
        scatter_dimension=0,
        tiled=True,
    ).astype(jnp.float32)
    peak_values = jnp.max(jnp.abs(waveforms.reshape(portion, gauge_count, NT)), axis=2)
    tile_total = coast_gauges.shape[0]
    slot_count = coast_gauges.shape[1]
    owners = lax.axis_size("rows")
    tiles_here = tile_total // owners
    active_slot = jnp.arange(slot_count, dtype=jnp.int32)[None, :] < coast_counts[:, None]
    weights = jnp.where(active_slot, coast_amps, jnp.zeros_like(coast_amps))
    gathered = lax.all_gather(peak_values, "rows", axis=1, tiled=True)
    first_tile = lax.axis_index("rows") * tiles_here
    mine_gauges = lax.dynamic_slice_in_dim(coast_gauges, first_tile, tiles_here, 0)
    mine_weights = lax.dynamic_slice_in_dim(weights, first_tile, tiles_here, 0)
    matches = (
        mine_gauges[:, :, None] == jnp.arange(gauge_count * owners, dtype=jnp.int32)[None, None, :]
    )
    tile_table = jnp.sum(jnp.where(matches, mine_weights[:, :, None], 0.0), axis=1)
    onshore = lax.dot_general(
        gathered,
        tile_table,
        (((1,), (1,)), ((), ())),
        precision=lax.Precision.HIGHEST,
        preferred_element_type=jnp.float32,
    )
    return onshore


def solution(mesh):
    in_specs = (P(None, "src"), P(None, "src"), P("src", "rows"), P(), P(), P())
    out_specs = P("src", "rows")
    return jax.shard_map(body, mesh=mesh, in_specs=in_specs, out_specs=out_specs, check_vma=False)
```

profile of v0, /device:TPU:2, one launch (start us, length us, event | category | flops | bytes accessed | tf_op | source)
XLA Modules:
  0.0 181.4 jit_solution(9424756790526116727)
XLA Ops:
  6.5 0.0 copy-start
  6.5 0.0 reduce-scatter.2.cloned.1.call-start
  6.5 2.4 %mul.14 = f32[512,8,125]{0,2,1:T(8,128)} broadcast(f32[512,8]{0,1:T(8,128)} %param.7), dimensions={0,1} | broadcast | bytes 2064384 | tf_op jit(solution)/shard_map/mul | solution.py:16
  8.9 1.8 %mul.15 = f32[512,1000]{0,1:T(8,128)S(1)} reshape(f32[512,8,125]{0,2,1:T(8,128)} %mul.14) | data formatting | bytes 4096000 | tf_op jit(solution)/shard_map/mul | solution.py:16
  10.8 10.0 %convolution_convert_fusion = bf16[512,3840]{1,0:T(8,128)(2,1)} fusion(bf16[1000,3840]{1,0:T(8,128)(2,1)} %param.8, f32[512,1000]{0,1:T(8,128)S(1)} %mul.15, s32[512,1000]{0,1:T(8,128)} %param.6), kind=kOutput, calls=%fused_computation.2 | convolution fusion | flops 3935662080 | bytes 15708160 | tf_op jit(solution)/shard_map/dot_general | solution.py:27
  20.8 0.0 reduce-scatter.2.cloned.1.call-update
  20.8 0.0 all-gather.2.cloned.1.call-start
  20.9 20.2 %reduce-scatter.2.cloned.1.call-done = bf16[256,3840]{1,0:T(8,128)(2,1)} async-done(((bf16[512,3840]{1,0:T(8,128)(2,1)}), bf16[256,3840]{1,0:T(8,128)(2,1)}) %reduce-scatter.2.cloned.1.call-update) | async-done | bytes 1966096 | tf_op jit(solution)/shard_map/reduce_scatter | solution.py:26
  41.1 3.7 %convert_abs_fusion = f32[256,3840]{1,0:T(8,128)} fusion(bf16[256,3840]{1,0:T(8,128)(2,1)} %reduce-scatter.2.cloned.1.call-done), kind=kLoop, calls=%fused_computation.3 | loop fusion | flops 1966080 | bytes 5898240 | tf_op jit(solution)/shard_map/abs | solution.py:32
  44.8 5.4 %copy.15 = f32[256,3840]{0,1:T(8,128)} copy(f32[256,3840]{1,0:T(8,128)} %convert_abs_fusion) | data formatting | bytes 7864320 | tf_op jit(solution)/shard_map/abs | solution.py:32
  50.3 3.0 %reduce_max.9 = f32[256,16]{0,1:T(8,128)} reduce(f32[256,16,240]{0,2,1:T(8,128)} %bitcast.6, f32[]{:T(128)} %constant.6.clone.1), dimensions={2}, to_apply=%region_1.0 | reduce | flops 978944 | bytes 3948548 | tf_op jit(solution)/shard_map/reduce_max | solution.py:32
  53.2 0.0 all-gather.2.cloned.1.call-update
  53.3 0.8 dynamic-slice
  54.0 0.7 dynamic-slice_select_fusion
  54.7 0.1 copy.17
  54.8 0.0 copy-done
  54.9 0.1 copy.16
  55.0 2.7 %select_reduce_fusion = f32[128,2048]{1,0:T(8,128)S(1)} fusion(f32[128,8]{1,0:T(8,128)S(1)} %copy.17, s32[128,8]{1,0:T(8,128)S(1)} %copy.16), kind=kLoop, calls=%fused_computation | loop fusion | flops 6029312 | bytes 1056768 | tf_op jit(solution)/shard_map/reduce_sum | solution.py:46
  57.7 111.2 %all-gather.2.cloned.1.call-done = f32[256,2048]{0,1:T(8,128)} async-done(((f32[256,16]{0,1:T(8,128)}), f32[256,2048]{0,1:T(8,128)}) %all-gather.2.cloned.1.call-update) | async-done | bytes 2097168 | tf_op jit(solution)/shard_map/all_gather | solution.py:39
  168.9 5.7 %fusion = f32[256,128]{1,0:T(8,128)} fusion(f32[256,2048]{0,1:T(8,128)} %all-gather.2.cloned.1.call-done, f32[128,2048]{1,0:T(8,128)S(1)} %select_reduce_fusion), kind=kOutput, calls=%fused_computation.8 | convolution fusion | flops 805306368 | bytes 3276800 | tf_op jit(solution)/shard_map/dot_general | solution.py:47
  (1 shorter events, 0.0 us)
Async XLA Ops:
  6.5 48.3 %copy-start = (s32[16384,8]{0,1:T(8,128)S(1)}, s32[16384,8]{0,1:T(8,128)}, u32[]{:S(2)}) copy-start(s32[16384,8]{0,1:T(8,128)} %param.9) | copy-start | bytes 1572868
  6.5 34.6 %reduce-scatter.2.cloned.1.call-start = ((), (), s32[]{:S(2)}) async-start(), calls=%async_computation.1 | async-start | bytes 5898240 | tf_op jit(solution)/shard_map/reduce_scatter | solution.py:26
  20.8 148.0 %all-gather.2.cloned.1.call-start = ((), (), s32[]{:S(2)}) async-start(), calls=%async_computation.2 | async-start | bytes 2113536 | tf_op jit(solution)/shard_map/all_gather | solution.py:39
Sparse Core Ops, SparseCore 0:
  20.9 20.1 reduce-scatter.1
  53.4 115.4 all-gather.1
where the time goes:
time: 182 us; the launch traced here: 181 us
  waiting for transfers between devices  131 us (72%)
  matrix products  15.7 us (9%)
  between operations  13.4 us (7%)
  local copies, waits for them, and re-layouts  10.7 us (6%)
  other arithmetic  10.1 us (6%)
    all_gather x1, waiting for transfers between devices, body(): gathered = lax.all_gather(peak_values, 'rows', axis=1, tiled=True)  111 us
    reduce_scatter x1, waiting for transfers between devices, body(): lax.psum_scatter(jnp.dot(slip_weights, green, preferred_element_type=jnp....  20.2 us
    dot_general x1, matrix products, body(): jnp.dot(slip_weights, green, preferred_element_type=jnp.float32)  10 us
    dot_general x1, matrix products, body(): lax.dot_general(gathered, tile_table, (((1,), (1,)), ((), ())), precision...  5.67 us
    abs x1, local copies, waits for them, and re-layouts, body(): jnp.abs(waveforms.reshape(portion, gauge_count, NT))  5.45 us
    mul x2, local copies, waits for them, and re-layouts, body(): slip_units.astype(jnp.float32).reshape(scenarios, block_count, UBLK)  4.23 us
    abs x1, other arithmetic, body(): jnp.abs(waveforms.reshape(portion, gauge_count, NT))  3.72 us
  transfers between devices with their start and end apart: 2, of which 2 were waited for; matrix products, arithmetic and copies ran while one was open for 2% of the time, Pallas kernels for 0%

commit v1 on v0

v1 whole, which is shorter than its diff:
```python
import functools

import jax
import jax.numpy as jnp
from jax import lax
from jax.experimental import pallas as pl
from jax.experimental.pallas import tpu as pltpu
from jax.sharding import PartitionSpec as P

NT = 240
UBLK = 125
NX, NY, NZ = 4, 4, 8
CHUNKS = 5
BF16 = jnp.bfloat16
F32 = jnp.float32
MESH = pl.DeviceIdType.MESH


def gauge_peaks(tiles, first, gauges, lane):
    peaks = []
    for g in range(first, first + gauges):
        start, end = g * NT, (g + 1) * NT
        best = None
        for tile in range(start // 128, (end + 127) // 128):
            value = tiles(tile)
            lo, hi = start - tile * 128, end - tile * 128
            if lo > 0:
                value = jnp.where(lane >= lo, value, jnp.zeros_like(value))
            if hi < 128:
                value = jnp.where(lane < hi, value, jnp.zeros_like(value))
            best = value if best is None else jnp.maximum(best, value)
        peaks.append(best)
    return peaks


def kernel(
    units_hbm, scales_ref, green_hbm, gauges_hbm, amps_hbm, counts_ref,
    out_ref,
    units, green, slip, own, outgoing, incoming, gathered, table,
    gauges, amps,
    load_sem, pair_send, pair_recv, z_send, z_recv, a_send, a_recv, b_send, b_recv,
):
    core = lax.axis_index("src")
    rank = lax.axis_index("rows")
    sources, columns = green.shape
    half = slip.shape[0] // 2
    width = columns // CHUNKS
    here = columns // NT
    tiles_here = out_ref.shape[1]
    total = gathered.shape[0]
    x, y, z = rank % NX, (rank // NX) % NY, rank // (NX * NY)
    a = jnp.where(core == 0, x, y)
    b = jnp.where(core == 0, y, x)

    def at(a_index, b_index, z_index):
        x_index = jnp.where(core == 0, a_index, b_index)
        y_index = jnp.where(core == 0, b_index, a_index)
        return (core, (z_index * NY + y_index) * NX + x_index)

    barrier = pltpu.get_barrier_semaphore()
    partners = [(1 - core, rank)]
    partners += [at(a, b, (z + d) % NZ) for d in range(1, NZ)]
    partners += [at((a + d) % NX, b, z) for d in range(1, NX)]
    partners += [at(a, (b + d) % NY, z) for d in range(1, NY)]
    for partner in partners:
        pl.semaphore_signal(barrier, inc=1, device_id=partner, device_id_type=MESH)

    loads = []
    load_units = pltpu.make_async_copy(units_hbm, units, load_sem.at[0])
    load_units.start()
    for n in range(CHUNKS):
        cols = pl.ds(n * width, width)
        copy = pltpu.make_async_copy(green_hbm.at[:, cols], green.at[:, cols], load_sem.at[1 + n])
        copy.start()
        loads.append(copy)
    tile_cols = pl.ds(pl.multiple_of(rank * tiles_here, 128), tiles_here)
    load_gauges = pltpu.make_async_copy(gauges_hbm.at[:, tile_cols], gauges, load_sem.at[1 + CHUNKS])
    load_amps = pltpu.make_async_copy(amps_hbm.at[:, tile_cols], amps, load_sem.at[2 + CHUNKS])
    load_gauges.start()
    load_amps.start()

    load_units.wait()
    blocks = scales_ref.shape[0]
    for i in range(blocks):
        low, high = i * 128, min(i * 128 + 128, sources)
        scale = scales_ref[i : i + 1, :]
        if i + 1 < blocks:
            row = lax.broadcasted_iota(jnp.int32, (high - low, 1), 0) + low
            scale = jnp.where(row < UBLK * (i + 1), scale, scales_ref[i + 1 : i + 2, :])
        piece = units[low:high, :].astype(F32) * scale
        slip[:, low:high] = piece.astype(BF16).T

    pair = []
    mine = pl.ds(pl.multiple_of(core * half, half), half)
    other = pl.ds(pl.multiple_of((1 - core) * half, half), half)
    for n in range(CHUNKS):
        cols = pl.ds(n * width, width)
        loads[n].wait()
        outgoing[:, cols] = jnp.dot(
            slip[other, :], green[:, cols], preferred_element_type=F32
        ).astype(BF16)
        if n == 0:
            pl.semaphore_wait(barrier, len(partners))
        copy = pltpu.make_async_remote_copy(
            src_ref=outgoing.at[:, cols],
            dst_ref=incoming.at[:, cols],
            send_sem=pair_send.at[n],
            recv_sem=pair_recv.at[n],
            device_id=(1 - core, rank),
            device_id_type=MESH,
        )
        copy.start()
        pair.append(copy)
        own[:, cols] = jnp.dot(
            slip[mine, :], green[:, cols], preferred_element_type=F32
        ).astype(BF16)

    load_gauges.wait()
    load_amps.wait()
    slots = gauges.shape[0]
    listed = gauges[...]
    owner = listed >> 4
    gauge_z = owner >> 4
    gauge_y = (owner >> 2) & 3
    gauge_x = owner & 3
    gauge_a = jnp.where(core == 0, gauge_x, gauge_y)
    gauge_b = jnp.where(core == 0, gauge_y, gauge_x)
    place = (((gauge_b * 4 + gauge_a) * 8 + gauge_z) * 16 + (listed & 15)).T
    slot = lax.broadcasted_iota(jnp.int32, (slots, 1), 0)
    count = counts_ref[pl.ds(rank, 1), :]
    weight = jnp.where(slot < count, amps[...], 0.0).T
    step = 256

    def fill(i, carry):
        first = pl.multiple_of(i * step, step)
        position = lax.broadcasted_iota(jnp.int32, (tiles_here, step), 1) + first
        value = jnp.zeros((tiles_here, step), F32)
        for k in range(slots):
            value += jnp.where(place[:, k : k + 1] == position, weight[:, k : k + 1], 0.0)
        high = value.astype(BF16)
        table[0:tiles_here, pl.ds(first, step)] = high
        table[tiles_here : 2 * tiles_here, pl.ds(first, step)] = (value - high.astype(F32)).astype(BF16)
        return carry

    lax.fori_loop(0, total // step, fill, 0)

    for copy in pair:
        copy.wait_recv()
    lane = lax.broadcasted_iota(jnp.int32, (half, 128), 1)

    def tiles(i):
        cols = pl.ds(i * 128, 128)
        return jnp.abs(own[:, cols].astype(F32) + incoming[:, cols].astype(F32))

    rows = []
    for best in gauge_peaks(tiles, 0, here, lane):
        rows.append(jnp.max(best.T, axis=0, keepdims=True))
    first = ((b * NX + a) * NZ + z) * here
    block = pl.ds(pl.multiple_of(first, here), here)
    gathered[block, :] = jnp.concatenate(rows, axis=0).astype(BF16)

    sent = []

    def spread(size, count, start_of, partner_of, send_sem, recv_sem):
        source = gathered.at[pl.ds(pl.multiple_of(start_of(0), size), size), :]
        copies = []
        for d in range(1, count):
            copy = pltpu.make_async_remote_copy(
                src_ref=source,
                dst_ref=source,
                send_sem=send_sem.at[d - 1],
                recv_sem=recv_sem.at[d - 1],
                device_id=partner_of(d),
                device_id_type=MESH,
            )
            copy.start()
            sent.append(copy)
        for d in range(1, count):
            landed = gathered.at[pl.ds(pl.multiple_of(start_of(-d), size), size), :]
            copies.append(
                pltpu.make_async_remote_copy(
                    src_ref=landed,
                    dst_ref=landed,
                    send_sem=send_sem.at[d - 1],
                    recv_sem=recv_sem.at[d - 1],
                    device_id=partner_of(d),
                    device_id_type=MESH,
                )
            )
        return copies

    arrivals = spread(
        here, NZ, lambda d: ((b * NX + a) * NZ + (z + d + NZ) % NZ) * here,
        lambda d: at(a, b, (z + d) % NZ), z_send, z_recv,
    )
    for copy in arrivals:
        copy.wait_recv()
    size = here * NZ
    arrivals = spread(
        size, NX, lambda d: (b * NX + (a + d + NX) % NX) * size,
        lambda d: at((a + d) % NX, b, z), a_send, a_recv,
    )
    for copy in arrivals:
        copy.wait_recv()
    size = size * NX
    arrivals = spread(
        size, NY, lambda d: ((b + d + NY) % NY) * size,
        lambda d: at(a, (b + d) % NY, z), b_send, b_recv,
    )
    for copy in arrivals:
        copy.wait_recv()

    both = jnp.dot(table[...], gathered[...], preferred_element_type=F32)
    out_ref[...] = (both[:tiles_here] + both[tiles_here:]).T
    for copy in pair + sent:
        copy.wait_send()


def body(slip_units, slip_scales, green, coast_gauges, coast_amps, coast_counts):
    scenarios, sources = slip_units.shape
    columns = green.shape[1]
    tile_total, slots = coast_gauges.shape
    owners = lax.axis_size("rows")
    tiles_here = tile_total // owners
    half = scenarios // lax.axis_size("src")
    total = columns // NT * owners
    hbm = pl.BlockSpec(memory_space=pl.ANY)
    vmem = pl.BlockSpec(memory_space=pltpu.VMEM)
    dma = pltpu.SemaphoreType.DMA
    return pl.pallas_call(
        kernel,
        out_shape=jax.ShapeDtypeStruct((half, tiles_here), F32),
        in_specs=[hbm, vmem, hbm, hbm, hbm, vmem],
        out_specs=vmem,
        scratch_shapes=[
            pltpu.VMEM((sources, scenarios), jnp.int32),
            pltpu.VMEM((sources, columns), BF16),
            pltpu.VMEM((scenarios, sources), BF16),
            pltpu.VMEM((half, columns), BF16),
            pltpu.VMEM((half, columns), BF16),
            pltpu.VMEM((half, columns), BF16),
            pltpu.VMEM((total, half), BF16),
            pltpu.VMEM((2 * tiles_here, total), BF16),
            pltpu.VMEM((slots, tiles_here), jnp.int32),
            pltpu.VMEM((slots, tiles_here), F32),
            dma((3 + CHUNKS,)),
            dma((CHUNKS,)),
            dma((CHUNKS,)),
            dma((NZ - 1,)),
            dma((NZ - 1,)),
            dma((NX - 1,)),
            dma((NX - 1,)),
            dma((NY - 1,)),
            dma((NY - 1,)),
        ],
        compiler_params=pltpu.CompilerParams(
            collective_id=0, has_side_effects=True, vmem_limit_bytes=56 * 1024 * 1024
        ),
    )(
        slip_units.T,
        slip_scales.T,
        green,
        coast_gauges.T,
        coast_amps.T,
        coast_counts.reshape(owners, tiles_here),
    )


def solution(mesh):
    in_specs = (P(None, "src"), P(None, "src"), P("src", "rows"), P(), P(), P())
    out_specs = P("src", "rows")
    return jax.shard_map(body, mesh=mesh, in_specs=in_specs, out_specs=out_specs, check_vma=False)
```

time: 182 us -> 42.2 us (0.23)
  the two profiles are of different devices: /device:TPU:2 before, /device:TPU:32 now
where the time goes in v1:
time: 42.2 us; the launch traced here: 42.1 us
  Pallas kernels  40.5 us (96%)
  local copies, waits for them, and re-layouts  1.57 us (4%)
    pallas_call x1, Pallas kernels, body(): pl.pallas_call(kernel, out_shape=jax.ShapeDtypeStruct((half, tiles_here),...  40.5 us
    unnamed x1, local copies, waits for them, and re-layouts  1.57 us

profile of v1, /device:TPU:32, one launch (start us, length us, event | category | flops | bytes accessed | tf_op | source)
XLA Modules:
  0.0 42.1 jit_solution(5831852119041549490)
XLA Ops:
  0.0 40.5 %shard_map.64 = f32[256,128]{1,0:T(8,128)} custom-call(s32[1000,512]{1,0:T(8,128)} %bitcast.5, f32[8,512]{1,0:T(8,128)} %bitcast.9, bf16[1000,3840]{1,0:T(8,128)(2,1)} %green_hbm.1, s32[8,16384]{1,0:T(8,128)} %bitcast.6, f32[8,16384]{1,0:T(8,128)} %bitcast.7, s32[128,128]{1,0:T(8,128)} %bitcast.8), custom_call_target="tpu_custom_call" | custom-call | tf_op jit(solution)/shard_map/pallas_call | solution.py:230
  40.5 1.6 %copy.8 = f32[256,128]{1,0:T(8,128)} copy(f32[256,128]{1,0:T(8,128)} %shard_map.64) | data formatting | bytes 262144

commit v2 on v1

v2 whole, which is shorter than its diff:
```python
import functools

import jax
import jax.numpy as jnp
from jax import lax
from jax.experimental import pallas as pl
from jax.experimental.pallas import tpu as pltpu
from jax.sharding import PartitionSpec as P

NT = 240
UBLK = 125
NX, NY, NZ = 4, 4, 8
NS_AXIS, NT_AXIS = 4, 4
DZ_ORDER = (4, 3, 5, 2, 6, 1, 7, 0)
CHUNKS = 5
HELD = 3
BF16 = jnp.bfloat16
F32 = jnp.float32
MESH = pl.DeviceIdType.MESH


def gauge_peaks(tiles, first, gauges, lane):
    peaks = []
    for g in range(first, first + gauges):
        start, end = g * NT, (g + 1) * NT
        best = None
        for tile in range(start // 128, (end + 127) // 128):
            value = tiles(tile)
            lo, hi = start - tile * 128, end - tile * 128
            if lo > 0:
                value = jnp.where(lane >= lo, value, jnp.zeros_like(value))
            if hi < 128:
                value = jnp.where(lane < hi, value, jnp.zeros_like(value))
            best = value if best is None else jnp.maximum(best, value)
        peaks.append(best)
    return peaks


def kernel(
    units_hbm, scales_ref, green_hbm, gauges_hbm, amps_hbm, counts_ref,
    out_ref,
    units, green, slip, own, outgoing, incoming, peaks, gathered, table,
    gauges, amps,
    load_sem, pair_send, pair_recv, plane_send, plane_recv, line_send, line_recv,
):
    core = lax.axis_index("src")
    rank = lax.axis_index("rows")
    sources, columns = green.shape
    half = slip.shape[0] // 2
    width = columns // CHUNKS
    here = columns // NT
    tiles_here = out_ref.shape[1]
    total = gathered.shape[0]
    x, y, z = rank % NX, (rank // NX) % NY, rank // (NX * NY)
    s = jnp.where(core == 0, x, y)
    t = jnp.where(core == 0, y, x)

    def at(s_index, t_index, z_index):
        x_index = jnp.where(core == 0, s_index, t_index)
        y_index = jnp.where(core == 0, t_index, s_index)
        return (core, (z_index * NY + y_index) * NX + x_index)

    load_units = pltpu.make_async_copy(units_hbm, units, load_sem.at[0])
    load_units.start()
    loads = []
    for n in range(CHUNKS):
        cols = pl.ds(n * width, width)
        copy = pltpu.make_async_copy(green_hbm.at[:, cols], green.at[:, cols], load_sem.at[1 + n])
        copy.start()
        loads.append(copy)
    tile_cols = pl.ds(pl.multiple_of(rank * tiles_here, 128), tiles_here)
    load_gauges = pltpu.make_async_copy(gauges_hbm.at[:, tile_cols], gauges, load_sem.at[1 + CHUNKS])
    load_amps = pltpu.make_async_copy(amps_hbm.at[:, tile_cols], amps, load_sem.at[2 + CHUNKS])
    load_gauges.start()
    load_amps.start()

    barrier = pltpu.get_barrier_semaphore()
    sibling = (1 - core, rank)
    plane = [
        at(s, (t + dt) % NT_AXIS, (z + dz) % NZ)
        for dz in DZ_ORDER for dt in range(NT_AXIS) if dz or dt
    ]
    line = [at((s + d) % NS_AXIS, t, z) for d in range(1, NS_AXIS)]
    partners = [sibling] + plane + line
    for partner in partners:
        pl.semaphore_signal(barrier, inc=1, device_id=partner, device_id_type=MESH)

    load_units.wait()
    blocks = scales_ref.shape[0]
    for i in range(blocks):
        low, high = i * 128, min(i * 128 + 128, sources)
        scale = scales_ref[i : i + 1, :]
        if i + 1 < blocks:
            row = lax.broadcasted_iota(jnp.int32, (high - low, 1), 0) + low
            scale = jnp.where(row < UBLK * (i + 1), scale, scales_ref[i + 1 : i + 2, :])
        piece = units[low:high, :].astype(F32) * scale
        slip[:, low:high] = piece.astype(BF16).T

    mine = pl.ds(pl.multiple_of(core * half, half), half)
    other = pl.ds(pl.multiple_of((1 - core) * half, half), half)
    pair = []
    for n in range(CHUNKS):
        cols = pl.ds(n * width, width)
        pair.append(
            pltpu.make_async_remote_copy(
                src_ref=outgoing.at[:, cols],
                dst_ref=incoming.at[:, cols],
                send_sem=pair_send.at[n],
                recv_sem=pair_recv.at[n],
                device_id=sibling,
                device_id_type=MESH,
            )
        )
    for n in range(CHUNKS):
        cols = pl.ds(n * width, width)
        loads[n].wait()
        outgoing[:, cols] = jnp.dot(
            slip[other, :], green[:, cols], preferred_element_type=F32
        ).astype(BF16)
        if n == HELD:
            pl.semaphore_wait(barrier, len(partners))
            for copy in pair[:HELD]:
                copy.start()
        if n >= HELD:
            pair[n].start()
    for n in range(CHUNKS):
        cols = pl.ds(n * width, width)
        own[:, cols] = jnp.dot(
            slip[mine, :], green[:, cols], preferred_element_type=F32
        ).astype(BF16)

    for copy in pair:
        copy.wait_recv()
    lane = lax.broadcasted_iota(jnp.int32, (half, 128), 1)

    def tiles(i):
        cols = pl.ds(i * 128, 128)
        return jnp.abs(own[:, cols].astype(F32) + incoming[:, cols].astype(F32))

    rows = []
    for best in gauge_peaks(tiles, 0, here, lane):
        rows.append(jnp.max(best.T, axis=0, keepdims=True))
    peaks[...] = jnp.concatenate(rows, axis=0).astype(BF16)

    def rows_of(index, size):
        return pl.ds(pl.multiple_of(index * size, size), size)

    block = gathered.at[rows_of((z * NS_AXIS + s) * NT_AXIS + t, here), :]
    place = z * NT_AXIS + t
    plane_copies = []
    for i, partner in enumerate(plane):
        copy = pltpu.make_async_remote_copy(
            src_ref=peaks,
            dst_ref=block,
            send_sem=plane_send.at[i],
            recv_sem=plane_recv.at[place],
            device_id=partner,
            device_id_type=MESH,
        )
        copy.start()
        plane_copies.append(copy)
    pltpu.make_async_copy(peaks, block, plane_recv.at[place]).start()

    load_gauges.wait()
    load_amps.wait()
    slots = gauges.shape[0]
    listed = gauges[...]
    owner = listed >> 4
    gauge_z = owner >> 4
    gauge_y = (owner >> 2) & 3
    gauge_x = owner & 3
    gauge_s = jnp.where(core == 0, gauge_x, gauge_y)
    gauge_t = jnp.where(core == 0, gauge_y, gauge_x)
    row = (((gauge_z * 4 + gauge_s) * 4 + gauge_t) * 16 + (listed & 15)).T
    slot = lax.broadcasted_iota(jnp.int32, (slots, 1), 0)
    count = counts_ref[pl.ds(rank, 1), :]
    weight = jnp.where(slot < count, amps[...], 0.0).T
    step = 256

    def fill(i, carry):
        first = pl.multiple_of(i * step, step)
        position = lax.broadcasted_iota(jnp.int32, (tiles_here, step), 1) + first
        value = jnp.zeros((tiles_here, step), F32)
        for k in range(slots):
            value += jnp.where(row[:, k : k + 1] == position, weight[:, k : k + 1], 0.0)
        high = value.astype(BF16)
        table[0:tiles_here, pl.ds(first, step)] = high
        table[tiles_here : 2 * tiles_here, pl.ds(first, step)] = (value - high.astype(F32)).astype(BF16)
        return carry

    lax.fori_loop(0, total // step, fill, 0)

    group = NT_AXIS * here
    line_copies = []
    for i in range(NZ):
        for j in range(NT_AXIS):
            landed = gathered.at[rows_of((i * NS_AXIS + s) * NT_AXIS + j, here), :]
            pltpu.make_async_copy(landed, landed, plane_recv.at[i * NT_AXIS + j]).wait()
        part = gathered.at[rows_of(i * NS_AXIS + s, group), :]
        for d in range(1, NS_AXIS):
            copy = pltpu.make_async_remote_copy(
                src_ref=part,
                dst_ref=part,
                send_sem=line_send.at[i * (NS_AXIS - 1) + d - 1],
                recv_sem=line_recv.at[i * (NS_AXIS - 1) + d - 1],
                device_id=line[d - 1],
                device_id_type=MESH,
            )
            copy.start()
            line_copies.append(copy)
    for copy in pair + plane_copies:
        copy.wait_send()

    depth = NS_AXIS * group
    both = jnp.zeros((2 * tiles_here, half), F32)
    for i in range(NZ):
        for d in range(1, NS_AXIS):
            landed = gathered.at[rows_of(i * NS_AXIS + (s + NS_AXIS - d) % NS_AXIS, group), :]
            pltpu.make_async_copy(
                landed, landed, line_recv.at[i * (NS_AXIS - 1) + d - 1]
            ).wait()
        cut = pl.ds(i * depth, depth)
        both += jnp.dot(table[:, cut], gathered[cut, :], preferred_element_type=F32)
    out_ref[...] = (both[:tiles_here] + both[tiles_here:]).T
    for copy in line_copies:
        copy.wait_send()


def body(slip_units, slip_scales, green, coast_gauges, coast_amps, coast_counts):
    scenarios, sources = slip_units.shape
    columns = green.shape[1]
    tile_total, slots = coast_gauges.shape
    owners = lax.axis_size("rows")
    tiles_here = tile_total // owners
    half = scenarios // lax.axis_size("src")
    total = columns // NT * owners
    hbm = pl.BlockSpec(memory_space=pl.ANY)
    vmem = pl.BlockSpec(memory_space=pltpu.VMEM)
    dma = pltpu.SemaphoreType.DMA
    return pl.pallas_call(
        kernel,
        out_shape=jax.ShapeDtypeStruct((half, tiles_here), F32),
        in_specs=[hbm, vmem, hbm, hbm, hbm, vmem],
        out_specs=vmem,
        scratch_shapes=[
            pltpu.VMEM((sources, scenarios), jnp.int32),
            pltpu.VMEM((sources, columns), BF16),
            pltpu.VMEM((scenarios, sources), BF16),
            pltpu.VMEM((half, columns), BF16),
            pltpu.VMEM((half, columns), BF16),
            pltpu.VMEM((half, columns), BF16),
            pltpu.VMEM((columns // NT, half), BF16),
            pltpu.VMEM((total, half), BF16),
            pltpu.VMEM((2 * tiles_here, total), BF16),
            pltpu.VMEM((slots, tiles_here), jnp.int32),
            pltpu.VMEM((slots, tiles_here), F32),
            dma((3 + CHUNKS,)),
            dma((CHUNKS,)),
            dma((CHUNKS,)),
            dma((NZ * NT_AXIS - 1,)),
            dma((NZ * NT_AXIS,)),
            dma((NZ * (NS_AXIS - 1),)),
            dma((NZ * (NS_AXIS - 1),)),
        ],
        compiler_params=pltpu.CompilerParams(
            collective_id=0, has_side_effects=True, vmem_limit_bytes=56 * 1024 * 1024
        ),
    )(
        slip_units.T,
        slip_scales.T,
        green,
        coast_gauges.T,
        coast_amps.T,
        coast_counts.reshape(owners, tiles_here),
    )


def solution(mesh):
    in_specs = (P(None, "src"), P(None, "src"), P("src", "rows"), P(), P(), P())
    out_specs = P("src", "rows")
    return jax.shard_map(body, mesh=mesh, in_specs=in_specs, out_specs=out_specs, check_vma=False)
```

time: 42.2 us -> 37.3 us (0.88)
  the two profiles are of different devices: /device:TPU:32 before, /device:TPU:1 now
where the time goes in v2:
time: 37.3 us; the launch traced here: 37.1 us
  Pallas kernels  35.5 us (95%)
  local copies, waits for them, and re-layouts  1.57 us (4%)
    pallas_call x1, Pallas kernels, body(): pl.pallas_call(kernel, out_shape=jax.ShapeDtypeStruct((half, tiles_here),...  35.5 us
    unnamed x1, local copies, waits for them, and re-layouts  1.57 us

profile of v2, /device:TPU:1, one launch (start us, length us, event | category | flops | bytes accessed | tf_op | source)
XLA Modules:
  0.0 37.1 jit_solution(10504699547192659231)
XLA Ops:
  0.0 35.5 %shard_map.64 = f32[256,128]{1,0:T(8,128)} custom-call(s32[1000,512]{1,0:T(8,128)} %bitcast.5, f32[8,512]{1,0:T(8,128)} %bitcast.9, bf16[1000,3840]{1,0:T(8,128)(2,1)} %green_hbm.1, s32[8,16384]{1,0:T(8,128)} %bitcast.6, f32[8,16384]{1,0:T(8,128)} %bitcast.7, s32[128,128]{1,0:T(8,128)} %bitcast.8), custom_call_target="tpu_custom_call" | custom-call | tf_op jit(solution)/shard_map/pallas_call | solution.py:240
  35.5 1.6 %copy.8 = f32[256,128]{1,0:T(8,128)} copy(f32[256,128]{1,0:T(8,128)} %shard_map.64) | data formatting | bytes 262144

commit v3 on v2

v3 whole, which is shorter than its diff:
```python
import functools

import jax
import jax.numpy as jnp
from jax import lax
from jax.experimental import pallas as pl
from jax.experimental.pallas import tpu as pltpu
from jax.sharding import PartitionSpec as P

NT = 240
UBLK = 125
NX, NY, NZ = 4, 4, 8
NS_AXIS, NT_AXIS = 4, 4
DZ_ORDER = (4, 3, 5, 2, 6, 1, 7, 0)
CHUNKS = 5
HELD = 2
PIECES = 2
BF16 = jnp.bfloat16
F32 = jnp.float32
MESH = pl.DeviceIdType.MESH


def gauge_peaks(tiles, first, gauges, lane):
    peaks = []
    for g in range(first, first + gauges):
        start, end = g * NT, (g + 1) * NT
        best = None
        for tile in range(start // 128, (end + 127) // 128):
            value = tiles(tile)
            lo, hi = start - tile * 128, end - tile * 128
            if lo > 0:
                value = jnp.where(lane >= lo, value, jnp.zeros_like(value))
            if hi < 128:
                value = jnp.where(lane < hi, value, jnp.zeros_like(value))
            best = value if best is None else jnp.maximum(best, value)
        peaks.append(best)
    return peaks


def kernel(
    units_hbm, scales_hbm, green_hbm, gauges_hbm, amps_hbm, counts_hbm,
    out_ref,
    units, green, slip, own, outgoing, incoming, peaks, gathered, table,
    scales, gauges, amps, counts,
    load_sem, pair_send, pair_recv, plane_send, plane_recv, line_send, line_recv,
):
    core = lax.axis_index("src")
    rank = lax.axis_index("rows")
    sources, columns = green.shape
    part = slip.shape[0] // 4
    width = columns // CHUNKS
    here = columns // NT
    tiles_here = out_ref.shape[1]
    total = gathered.shape[1]
    x, y, z = rank % NX, (rank // NX) % NY, rank // (NX * NY)
    s = jnp.where(core == 0, x, y)
    t = jnp.where(core == 0, y, x)

    def at(s_index, t_index, z_index):
        x_index = jnp.where(core == 0, s_index, t_index)
        y_index = jnp.where(core == 0, t_index, s_index)
        return (core, (z_index * NY + y_index) * NX + x_index)

    tile_cols = pl.ds(pl.multiple_of(rank * tiles_here, 128), tiles_here)
    load_gauges = pltpu.make_async_copy(gauges_hbm.at[:, tile_cols], gauges, load_sem.at[1 + CHUNKS])
    load_amps = pltpu.make_async_copy(amps_hbm.at[:, tile_cols], amps, load_sem.at[2 + CHUNKS])
    load_gauges.start()
    load_amps.start()
    load_counts = pltpu.make_async_copy(counts_hbm, counts, load_sem.at[4 + CHUNKS])
    load_counts.start()
    load_units = pltpu.make_async_copy(units_hbm, units, load_sem.at[0])
    load_units.start()
    load_scales = pltpu.make_async_copy(scales_hbm, scales, load_sem.at[3 + CHUNKS])
    load_scales.start()
    loads = []
    for n in range(CHUNKS):
        cols = pl.ds(n * width, width)
        copy = pltpu.make_async_copy(green_hbm.at[:, cols], green.at[:, cols], load_sem.at[1 + n])
        copy.start()
        loads.append(copy)

    barrier = pltpu.get_barrier_semaphore()
    sibling = (1 - core, rank)
    plane = [
        at(s, (t + dt) % NT_AXIS, (z + dz) % NZ)
        for dz in DZ_ORDER for dt in range(NT_AXIS) if dz or dt
    ]
    line = [at((s + d) % NS_AXIS, t, z) for d in range(1, NS_AXIS)]
    partners = [sibling] + plane + line
    for partner in partners:
        pl.semaphore_signal(barrier, inc=1, device_id=partner, device_id_type=MESH)

    load_gauges.wait()
    load_amps.wait()
    load_counts.wait()
    slots = gauges.shape[0]
    listed = gauges[...]
    owner = listed >> 4
    gauge_z = owner >> 4
    gauge_y = (owner >> 2) & 3
    gauge_x = owner & 3
    gauge_s = jnp.where(core == 0, gauge_x, gauge_y)
    gauge_t = jnp.where(core == 0, gauge_y, gauge_x)
    row = (((gauge_z * 4 + gauge_s) * 4 + gauge_t) * 16 + (listed & 15)).T
    slot = lax.broadcasted_iota(jnp.int32, (slots, 1), 0)
    count = counts[pl.ds(rank, 1), :]
    weight = jnp.where(slot < count, amps[...], 0.0).T
    step = 256

    def fill(i, carry):
        first = pl.multiple_of(i * step, step)
        position = lax.broadcasted_iota(jnp.int32, (tiles_here, step), 1) + first
        value = jnp.zeros((tiles_here, step), F32)
        for k in range(slots):
            value += jnp.where(row[:, k : k + 1] == position, weight[:, k : k + 1], 0.0)
        high = value.astype(BF16)
        table[0:tiles_here, pl.ds(first, step)] = high
        table[tiles_here : 2 * tiles_here, pl.ds(first, step)] = (value - high.astype(F32)).astype(BF16)
        return carry

    lax.fori_loop(0, total // step, fill, 0)

    load_scales.wait()
    load_units.wait()
    blocks = scales.shape[0]
    for i in range(blocks):
        low, high = i * 128, min(i * 128 + 128, sources)
        scale = scales[i : i + 1, :]
        if i + 1 < blocks:
            source = lax.broadcasted_iota(jnp.int32, (high - low, 1), 0) + low
            scale = jnp.where(source < UBLK * (i + 1), scale, scales[i + 1 : i + 2, :])
        piece = units[low:high, :].astype(F32) * scale
        slip[:, low:high] = piece.astype(BF16).T

    other = pl.ds(pl.multiple_of((1 - core) * 2 * part, 2 * part), 2 * part)

    def to_sibling(h, n):
        cols = pl.ds(n * width, width)
        pltpu.make_async_remote_copy(
            src_ref=outgoing.at[h, :, cols],
            dst_ref=incoming.at[h, :, cols],
            send_sem=pair_send.at[h],
            recv_sem=pair_recv.at[h],
            device_id=sibling,
            device_id_type=MESH,
        ).start()

    for n in range(CHUNKS):
        cols = pl.ds(n * width, width)
        loads[n].wait()
        value = jnp.dot(slip[other, :], green[:, cols], preferred_element_type=F32).astype(BF16)
        outgoing[0, :, cols] = value[:part]
        outgoing[1, :, cols] = value[part:]
        if n == HELD:
            pl.semaphore_wait(barrier, len(partners))
            for h in range(2):
                for m in range(HELD):
                    to_sibling(h, m)
        if n >= HELD:
            for h in range(2):
                to_sibling(h, n)

    def rows_of(index, size):
        return pl.ds(pl.multiple_of(index * size, size), size)

    lane = lax.broadcasted_iota(jnp.int32, (part, 128), 1)
    for h in range(2):
        mine = rows_of(core * 2 + h, part)
        for n in range(CHUNKS):
            cols = pl.ds(n * width, width)
            own[h, :, cols] = jnp.dot(
                slip[mine, :], green[:, cols], preferred_element_type=F32
            ).astype(BF16)
        pltpu.make_async_copy(incoming.at[h], incoming.at[h], pair_recv.at[h]).wait()

        def tiles(i):
            cols = pl.ds(i * 128, 128)
            return jnp.abs(own[h, :, cols].astype(F32) + incoming[h, :, cols].astype(F32))

        highest = []
        for best in gauge_peaks(tiles, 0, here, lane):
            highest.append(jnp.max(best.T, axis=0, keepdims=True))
        peaks[h] = jnp.concatenate(highest, axis=0).astype(BF16)
        block = gathered.at[h, rows_of((z * NS_AXIS + s) * NT_AXIS + t, here), :]
        for partner in plane:
            pltpu.make_async_remote_copy(
                src_ref=peaks.at[h],
                dst_ref=block,
                send_sem=plane_send.at[h],
                recv_sem=plane_recv.at[h * NZ + z],
                device_id=partner,
                device_id_type=MESH,
            ).start()
        pltpu.make_async_copy(peaks.at[h], block, plane_recv.at[h * NZ + z]).start()

    group = NT_AXIS * here
    for h in range(2):
        for i in range(NZ):
            whole = gathered.at[h, rows_of(i * NS_AXIS + s, group), :]
            pltpu.make_async_copy(whole, whole, plane_recv.at[h * NZ + i]).wait()
            for d in range(1, NS_AXIS):
                pltpu.make_async_remote_copy(
                    src_ref=whole,
                    dst_ref=whole,
                    send_sem=line_send.at[h],
                    recv_sem=line_recv.at[h * NZ + i],
                    device_id=line[d - 1],
                    device_id_type=MESH,
                ).start()

    depth = NS_AXIS * group
    cut = depth * NZ // PIECES
    for h in range(2):
        both = jnp.zeros((2 * tiles_here, part), F32)
        for i in range(NZ):
            landed = gathered.at[h, pl.ds(i * depth, depth - group), :]
            pltpu.make_async_copy(landed, landed, line_recv.at[h * NZ + i]).wait()
            if (i + 1) % (NZ // PIECES) == 0:
                piece = pl.ds((i + 1) * depth - cut, cut)
                both += jnp.dot(table[:, piece], gathered[h, piece, :], preferred_element_type=F32)
        out_ref[h * part : (h + 1) * part, :] = (both[:tiles_here] + both[tiles_here:]).T

    for h in range(2):
        pltpu.make_async_copy(outgoing.at[h], outgoing.at[h], pair_send.at[h]).wait()
        sent = gathered.at[h, pl.ds(0, len(plane) * here), :]
        pltpu.make_async_copy(sent, sent, plane_send.at[h]).wait()
        sent = gathered.at[h, pl.ds(0, (NS_AXIS - 1) * group * NZ), :]
        pltpu.make_async_copy(sent, sent, line_send.at[h]).wait()


def body(slip_units, slip_scales, green, coast_gauges, coast_amps, coast_counts):
    scenarios, sources = slip_units.shape
    columns = green.shape[1]
    tile_total, slots = coast_gauges.shape
    owners = lax.axis_size("rows")
    tiles_here = tile_total // owners
    half = scenarios // lax.axis_size("src")
    total = columns // NT * owners
    hbm = pl.BlockSpec(memory_space=pl.ANY)
    vmem = pl.BlockSpec(memory_space=pltpu.VMEM)
    dma = pltpu.SemaphoreType.DMA
    return pl.pallas_call(
        kernel,
        out_shape=jax.ShapeDtypeStruct((half, tiles_here), F32),
        in_specs=[hbm] * 6,
        out_specs=vmem,
        scratch_shapes=[
            pltpu.VMEM((sources, scenarios), jnp.int32),
            pltpu.VMEM((sources, columns), BF16),
            pltpu.VMEM((scenarios, sources), BF16),
            pltpu.VMEM((2, half // 2, columns), BF16),
            pltpu.VMEM((2, half // 2, columns), BF16),
            pltpu.VMEM((2, half // 2, columns), BF16),
            pltpu.VMEM((2, columns // NT, half // 2), BF16),
            pltpu.VMEM((2, total, half // 2), BF16),
            pltpu.VMEM((2 * tiles_here, total), BF16),
            pltpu.VMEM(slip_scales.shape[::-1], F32),
            pltpu.VMEM((slots, tiles_here), jnp.int32),
            pltpu.VMEM((slots, tiles_here), F32),
            pltpu.VMEM((owners, tiles_here), jnp.int32),
            dma((5 + CHUNKS,)),
            dma((2,)),
            dma((2,)),
            dma((2,)),
            dma((2 * NZ,)),
            dma((2,)),
            dma((2 * NZ,)),
        ],
        compiler_params=pltpu.CompilerParams(
            collective_id=0, has_side_effects=True, vmem_limit_bytes=58 * 1024 * 1024
        ),
    )(
        slip_units.T,
        slip_scales.T,
        green,
        coast_gauges.T,
        coast_amps.T,
        coast_counts.reshape(owners, tiles_here),
    )


def solution(mesh):
    in_specs = (P(None, "src"), P(None, "src"), P("src", "rows"), P(), P(), P())
    out_specs = P("src", "rows")
    return jax.shard_map(body, mesh=mesh, in_specs=in_specs, out_specs=out_specs, check_vma=False)
```

time: 37.3 us -> 34.7 us (0.930)
  Pallas kernels: 35.5 us -> 33.1 us
    pallas_call x1, Pallas kernels: 35.5 us -> 33.1 us  [body(): pl.pallas_call(kernel, out_shape=jax.ShapeDtypeStruct((half, tiles_here),...]
where the time goes in v3:
time: 34.7 us; the launch traced here: 34.6 us
  Pallas kernels  33.1 us (95%)
  local copies, waits for them, and re-layouts  1.57 us (5%)
    pallas_call x1, Pallas kernels, body(): pl.pallas_call(kernel, out_shape=jax.ShapeDtypeStruct((half, tiles_here),...  33.1 us
    unnamed x1, local copies, waits for them, and re-layouts  1.57 us

profile of v3, /device:TPU:1, one launch (start us, length us, event | category | flops | bytes accessed | tf_op | source)
XLA Modules:
  0.0 34.6 jit_solution(2088195749078667678)
XLA Ops:
  0.0 33.1 %shard_map.64 = f32[256,128]{1,0:T(8,128)} custom-call(s32[1000,512]{1,0:T(8,128)} %bitcast.5, f32[8,512]{1,0:T(8,128)} %bitcast.9, bf16[1000,3840]{1,0:T(8,128)(2,1)} %green_hbm.1, s32[8,16384]{1,0:T(8,128)} %bitcast.6, f32[8,16384]{1,0:T(8,128)} %bitcast.7, s32[128,128]{1,0:T(8,128)} %bitcast.8), custom_call_target="tpu_custom_call" | custom-call | tf_op jit(solution)/shard_map/pallas_call | solution.py:242
  33.1 1.6 %copy.8 = f32[256,128]{1,0:T(8,128)} copy(f32[256,128]{1,0:T(8,128)} %shard_map.64) | data formatting | bytes 262144

commit v4 on v3

--- a/solution.py
+++ b/solution.py
@@ -11,9 +11,8 @@
 UBLK = 125
 NX, NY, NZ = 4, 4, 8
 NS_AXIS, NT_AXIS = 4, 4
-DZ_ORDER = (4, 3, 5, 2, 6, 1, 7, 0)
 CHUNKS = 5
-HELD = 2
+HELD = 1
 PIECES = 2
 BF16 = jnp.bfloat16
 F32 = jnp.float32
@@ -81,14 +80,101 @@
 
     barrier = pltpu.get_barrier_semaphore()
     sibling = (1 - core, rank)
-    plane = [
-        at(s, (t + dt) % NT_AXIS, (z + dz) % NZ)
-        for dz in DZ_ORDER for dt in range(NT_AXIS) if dz or dt
-    ]
-    line = [at((s + d) % NS_AXIS, t, z) for d in range(1, NS_AXIS)]
+    offsets = [(dz, dt) for dz in range(NZ) for dt in range(NT_AXIS) if dz or dt]
+    offsets.sort(key=lambda o: -(min(o[0], NZ - o[0]) + min(o[1], NT_AXIS - o[1])))
+    plane = [at(s, (t + dt) % NT_AXIS, (z + dz) % NZ) for dz, dt in offsets]
+    line = [at((s + d) % NS_AXIS, t, z) for d in (2, 1, 3)]
     partners = [sibling] + plane + line
     for partner in partners:
         pl.semaphore_signal(barrier, inc=1, device_id=partner, device_id_type=MESH)
+
+    load_scales.wait()
+    load_units.wait()
+    blocks = scales.shape[0]
+    for i in range(blocks):
+        low, high = i * 128, min(i * 128 + 128, sources)
+        scale = scales[i : i + 1, :]
+        if i + 1 < blocks:
+            source = lax.broadcasted_iota(jnp.int32, (high - low, 1), 0) + low
+            scale = jnp.where(source < UBLK * (i + 1), scale, scales[i + 1 : i + 2, :])
+        piece = units[low:high, :].astype(F32) * scale
+        slip[:, low:high] = piece.astype(BF16).T
+
+    other = pl.ds(pl.multiple_of((1 - core) * 2 * part, 2 * part), 2 * part)
+
+    def to_sibling(h, n):
+        cols = pl.ds(n * width, width)
+        pltpu.make_async_remote_copy(
+            src_ref=outgoing.at[h, :, cols],
+            dst_ref=incoming.at[h, :, cols],
+            send_sem=pair_send.at[h],
+            recv_sem=pair_recv.at[h],
+            device_id=sibling,
+            device_id_type=MESH,
+        ).start()
+
+    for n in range(CHUNKS):
+        cols = pl.ds(n * width, width)
+        loads[n].wait()
+        value = jnp.dot(slip[other, :], green[:, cols], preferred_element_type=F32).astype(BF16)
+        outgoing[0, :, cols] = value[:part]
+        outgoing[1, :, cols] = value[part:]
+        if n == HELD:
+            pl.semaphore_wait(barrier, len(partners))
+            for h in range(2):
+                for m in range(HELD):
+                    to_sibling(h, m)
+        if n >= HELD:
+            for h in range(2):
+                to_sibling(h, n)
+
+    def rows_of(index, size):
+        return pl.ds(pl.multiple_of(index * size, size), size)
+
+    lane = lax.broadcasted_iota(jnp.int32, (part, 128), 1)
+    for h in range(2):
+        mine = rows_of(core * 2 + h, part)
+        for n in range(CHUNKS):
+            cols = pl.ds(n * width, width)
+            own[h, :, cols] = jnp.dot(
+                slip[mine, :], green[:, cols], preferred_element_type=F32
+            ).astype(BF16)
+        pltpu.make_async_copy(incoming.at[h], incoming.at[h], pair_recv.at[h]).wait()
+
+        def tiles(i):
+            cols = pl.ds(i * 128, 128)
+            return jnp.abs(own[h, :, cols].astype(F32) + incoming[h, :, cols].astype(F32))
+
+        highest = []
+        for best in gauge_peaks(tiles, 0, here, lane):
+            highest.append(jnp.max(best.T, axis=0, keepdims=True))
+        peaks[h] = jnp.concatenate(highest, axis=0).astype(BF16)
+        block = gathered.at[h, rows_of((z * NS_AXIS + s) * NT_AXIS + t, here), :]
+        for partner in plane:
+            pltpu.make_async_remote_copy(
+                src_ref=peaks.at[h],
+                dst_ref=block,
+                send_sem=plane_send.at[h],
+                recv_sem=plane_recv.at[h * NZ + z],
+                device_id=partner,
+                device_id_type=MESH,
+            ).start()
+        pltpu.make_async_copy(peaks.at[h], block, plane_recv.at[h * NZ + z]).start()
+
+    group = NT_AXIS * here
+    for h in range(2):
+        for i in range(NZ):
+            whole = gathered.at[h, rows_of(i * NS_AXIS + s, group), :]
+            pltpu.make_async_copy(whole, whole, plane_recv.at[h * NZ + i]).wait()
+            for partner in line:
+                pltpu.make_async_remote_copy(
+                    src_ref=whole,
+                    dst_ref=whole,
+                    send_sem=line_send.at[h],
+                    recv_sem=line_recv.at[h * NZ + i],
+                    device_id=partner,
+                    device_id_type=MESH,
+                ).start()
 
     load_gauges.wait()
     load_amps.wait()
@@ -119,94 +205,6 @@
         return carry
 
     lax.fori_loop(0, total // step, fill, 0)
-
-    load_scales.wait()
-    load_units.wait()
-    blocks = scales.shape[0]
-    for i in range(blocks):
-        low, high = i * 128, min(i * 128 + 128, sources)
-        scale = scales[i : i + 1, :]
-        if i + 1 < blocks:
-            source = lax.broadcasted_iota(jnp.int32, (high - low, 1), 0) + low
-            scale = jnp.where(source < UBLK * (i + 1), scale, scales[i + 1 : i + 2, :])
-        piece = units[low:high, :].astype(F32) * scale
-        slip[:, low:high] = piece.astype(BF16).T
-
-    other = pl.ds(pl.multiple_of((1 - core) * 2 * part, 2 * part), 2 * part)
-
-    def to_sibling(h, n):
-        cols = pl.ds(n * width, width)
-        pltpu.make_async_remote_copy(
-            src_ref=outgoing.at[h, :, cols],
-            dst_ref=incoming.at[h, :, cols],
-            send_sem=pair_send.at[h],
-            recv_sem=pair_recv.at[h],
-            device_id=sibling,
-            device_id_type=MESH,
-        ).start()
-
-    for n in range(CHUNKS):
-        cols = pl.ds(n * width, width)
-        loads[n].wait()
-        value = jnp.dot(slip[other, :], green[:, cols], preferred_element_type=F32).astype(BF16)
-        outgoing[0, :, cols] = value[:part]
-        outgoing[1, :, cols] = value[part:]
-        if n == HELD:
-            pl.semaphore_wait(barrier, len(partners))
-            for h in range(2):
-                for m in range(HELD):
-                    to_sibling(h, m)
-        if n >= HELD:
-            for h in range(2):
-                to_sibling(h, n)
-
-    def rows_of(index, size):
-        return pl.ds(pl.multiple_of(index * size, size), size)
-
-    lane = lax.broadcasted_iota(jnp.int32, (part, 128), 1)
-    for h in range(2):
-        mine = rows_of(core * 2 + h, part)
-        for n in range(CHUNKS):
-            cols = pl.ds(n * width, width)
-            own[h, :, cols] = jnp.dot(
-                slip[mine, :], green[:, cols], preferred_element_type=F32
-            ).astype(BF16)
-        pltpu.make_async_copy(incoming.at[h], incoming.at[h], pair_recv.at[h]).wait()
-
-        def tiles(i):
-            cols = pl.ds(i * 128, 128)
-            return jnp.abs(own[h, :, cols].astype(F32) + incoming[h, :, cols].astype(F32))
-
-        highest = []
-        for best in gauge_peaks(tiles, 0, here, lane):
-            highest.append(jnp.max(best.T, axis=0, keepdims=True))
-        peaks[h] = jnp.concatenate(highest, axis=0).astype(BF16)
-        block = gathered.at[h, rows_of((z * NS_AXIS + s) * NT_AXIS + t, here), :]
-        for partner in plane:
-            pltpu.make_async_remote_copy(
-                src_ref=peaks.at[h],
-                dst_ref=block,
-                send_sem=plane_send.at[h],
-                recv_sem=plane_recv.at[h * NZ + z],
-                device_id=partner,
-                device_id_type=MESH,
-            ).start()
-        pltpu.make_async_copy(peaks.at[h], block, plane_recv.at[h * NZ + z]).start()
-
-    group = NT_AXIS * here
-    for h in range(2):
-        for i in range(NZ):
-            whole = gathered.at[h, rows_of(i * NS_AXIS + s, group), :]
-            pltpu.make_async_copy(whole, whole, plane_recv.at[h * NZ + i]).wait()
-            for d in range(1, NS_AXIS):
-                pltpu.make_async_remote_copy(
-                    src_ref=whole,
-                    dst_ref=whole,
-                    send_sem=line_send.at[h],
-                    recv_sem=line_recv.at[h * NZ + i],
-                    device_id=line[d - 1],
-                    device_id_type=MESH,
-                ).start()
 
     depth = NS_AXIS * group
     cut = depth * NZ // PIECES

time: 34.7 us -> 32.1 us (0.925)
  the two profiles are of different devices: /device:TPU:1 before, /device:TPU:2 now
where the time goes in v4:
time: 32.1 us; the launch traced here: 31.5 us
  Pallas kernels  29.9 us (93%)
  local copies, waits for them, and re-layouts  1.57 us (5%)
    pallas_call x1, Pallas kernels, body(): pl.pallas_call(kernel, out_shape=jax.ShapeDtypeStruct((half, tiles_here),...  29.9 us
    unnamed x1, local copies, waits for them, and re-layouts  1.57 us

profile of v4, /device:TPU:2, one launch (start us, length us, event | category | flops | bytes accessed | tf_op | source)
XLA Modules:
  0.0 31.5 jit_solution(12599415444370167386)
XLA Ops:
  0.0 29.9 %shard_map.64 = f32[256,128]{1,0:T(8,128)} custom-call(s32[1000,512]{1,0:T(8,128)} %bitcast.5, f32[8,512]{1,0:T(8,128)} %bitcast.9, bf16[1000,3840]{1,0:T(8,128)(2,1)} %green_hbm.1, s32[8,16384]{1,0:T(8,128)} %bitcast.6, f32[8,16384]{1,0:T(8,128)} %bitcast.7, s32[128,128]{1,0:T(8,128)} %bitcast.8), custom_call_target="tpu_custom_call" | custom-call | tf_op jit(solution)/shard_map/pallas_call | solution.py:240
  29.9 1.6 %copy.8 = f32[256,128]{1,0:T(8,128)} copy(f32[256,128]{1,0:T(8,128)} %shard_map.64) | data formatting | bytes 262144

commit v5 on v4

--- a/solution.py
+++ b/solution.py
@@ -12,8 +12,8 @@
 NX, NY, NZ = 4, 4, 8
 NS_AXIS, NT_AXIS = 4, 4
 CHUNKS = 5
-HELD = 1
-PIECES = 2
+HELD = 2
+PIECES = 4
 BF16 = jnp.bfloat16
 F32 = jnp.float32
 MESH = pl.DeviceIdType.MESH
@@ -121,12 +121,12 @@
         outgoing[1, :, cols] = value[part:]
         if n == HELD:
             pl.semaphore_wait(barrier, len(partners))
-            for h in range(2):
-                for m in range(HELD):
-                    to_sibling(h, m)
+            for m in range(HELD):
+                to_sibling(0, m)
         if n >= HELD:
-            for h in range(2):
-                to_sibling(h, n)
+            to_sibling(0, n)
+    for n in range(CHUNKS):
+        to_sibling(1, n)
 
     def rows_of(index, size):
         return pl.ds(pl.multiple_of(index * size, size), size)
@@ -143,11 +143,16 @@
 
         def tiles(i):
             cols = pl.ds(i * 128, 128)
-            return jnp.abs(own[h, :, cols].astype(F32) + incoming[h, :, cols].astype(F32))
+            value = own[h, :, cols].astype(F32) + incoming[h, :, cols].astype(F32)
+            return jnp.abs(value).astype(BF16)
 
         highest = []
         for best in gauge_peaks(tiles, 0, here, lane):
-            highest.append(jnp.max(best.T, axis=0, keepdims=True))
+            turned = best.T
+            top = turned[0:16]
+            for i in range(16, 128, 16):
+                top = jnp.maximum(top, turned[i : i + 16])
+            highest.append(jnp.max(top.astype(F32), axis=0, keepdims=True))
         peaks[h] = jnp.concatenate(highest, axis=0).astype(BF16)
         block = gathered.at[h, rows_of((z * NS_AXIS + s) * NT_AXIS + t, here), :]
         for partner in plane:

time: 32.1 us -> 31.2 us (0.972); the launches traced: 31.5 us -> 31.1 us
    pallas_call x1, Pallas kernels: 29.9 us -> 29.6 us  [body(): pl.pallas_call(kernel, out_shape=jax.ShapeDtypeStruct((half, tiles_here),...]
where the time goes in v5:
time: 31.2 us; the launch traced here: 31.1 us
  Pallas kernels  29.6 us (95%)
  local copies, waits for them, and re-layouts  1.57 us (5%)
    pallas_call x1, Pallas kernels, body(): pl.pallas_call(kernel, out_shape=jax.ShapeDtypeStruct((half, tiles_here),...  29.6 us
    unnamed x1, local copies, waits for them, and re-layouts  1.57 us

profile of v5, /device:TPU:2, one launch (start us, length us, event | category | flops | bytes accessed | tf_op | source)
XLA Modules:
  0.0 31.1 jit_solution(4350732908578981595)
XLA Ops:
  0.0 29.6 %shard_map.64 = f32[256,128]{1,0:T(8,128)} custom-call(s32[1000,512]{1,0:T(8,128)} %bitcast.5, f32[8,512]{1,0:T(8,128)} %bitcast.9, bf16[1000,3840]{1,0:T(8,128)(2,1)} %green_hbm.1, s32[8,16384]{1,0:T(8,128)} %bitcast.6, f32[8,16384]{1,0:T(8,128)} %bitcast.7, s32[128,128]{1,0:T(8,128)} %bitcast.8), custom_call_target="tpu_custom_call" | custom-call | tf_op jit(solution)/shard_map/pallas_call | solution.py:245
  29.6 1.6 %copy.8 = f32[256,128]{1,0:T(8,128)} copy(f32[256,128]{1,0:T(8,128)} %shard_map.64) | data formatting | bytes 262144

commit v6 on v5

--- a/solution.py
+++ b/solution.py
@@ -67,8 +67,13 @@
     load_amps.start()
     load_counts = pltpu.make_async_copy(counts_hbm, counts, load_sem.at[4 + CHUNKS])
     load_counts.start()
-    load_units = pltpu.make_async_copy(units_hbm, units, load_sem.at[0])
-    load_units.start()
+    load_units = []
+    for i, (low, high) in enumerate(((0, 512), (512, sources))):
+        copy = pltpu.make_async_copy(
+            units_hbm.at[low:high, :], units.at[low:high, :], load_sem.at[(5 + CHUNKS) * i]
+        )
+        copy.start()
+        load_units.append(copy)
     load_scales = pltpu.make_async_copy(scales_hbm, scales, load_sem.at[3 + CHUNKS])
     load_scales.start()
     loads = []
@@ -89,10 +94,12 @@
         pl.semaphore_signal(barrier, inc=1, device_id=partner, device_id_type=MESH)
 
     load_scales.wait()
-    load_units.wait()
+    load_units[0].wait()
     blocks = scales.shape[0]
     for i in range(blocks):
         low, high = i * 128, min(i * 128 + 128, sources)
+        if low == 512:
+            load_units[1].wait()
         scale = scales[i : i + 1, :]
         if i + 1 < blocks:
             source = lax.broadcasted_iota(jnp.int32, (high - low, 1), 0) + low
@@ -261,7 +268,7 @@
             pltpu.VMEM((slots, tiles_here), jnp.int32),
             pltpu.VMEM((slots, tiles_here), F32),
             pltpu.VMEM((owners, tiles_here), jnp.int32),
-            dma((5 + CHUNKS,)),
+            dma((6 + CHUNKS,)),
             dma((2,)),
             dma((2,)),
             dma((2,)),

time: 31.2 us -> 31.2 us (level)
  no operation moved by 1% of the time
where the time goes in v6:
time: 31.2 us; the launch traced here: 31.1 us
  Pallas kernels  29.6 us (95%)
  local copies, waits for them, and re-layouts  1.57 us (5%)
    pallas_call x1, Pallas kernels, body(): pl.pallas_call(kernel, out_shape=jax.ShapeDtypeStruct((half, tiles_here),...  29.6 us
    unnamed x1, local copies, waits for them, and re-layouts  1.57 us

profile of v6, /device:TPU:2, one launch (start us, length us, event | category | flops | bytes accessed | tf_op | source)
XLA Modules:
  0.0 31.1 jit_solution(18064110660037380423)
XLA Ops:
  0.0 29.6 %shard_map.64 = f32[256,128]{1,0:T(8,128)} custom-call(s32[1000,512]{1,0:T(8,128)} %bitcast.5, f32[8,512]{1,0:T(8,128)} %bitcast.9, bf16[1000,3840]{1,0:T(8,128)(2,1)} %green_hbm.1, s32[8,16384]{1,0:T(8,128)} %bitcast.6, f32[8,16384]{1,0:T(8,128)} %bitcast.7, s32[128,128]{1,0:T(8,128)} %bitcast.8), custom_call_target="tpu_custom_call" | custom-call | tf_op jit(solution)/shard_map/pallas_call | solution.py:252
  29.6 1.6 %copy.8 = f32[256,128]{1,0:T(8,128)} copy(f32[256,128]{1,0:T(8,128)} %shard_map.64) | data formatting | bytes 262144
